TPU v7x, 32 devices: a whole 2x2x4 slice. The times are simulated.
32 devices in a mesh: grp: 2 (over core), aux: 4 (over y, x), orb: 4 (over z).
Axes of the slice: x: 2, y: 2, z: 4, core: 2. Of those that a mesh axis runs over, the one named last changes fastest.
Arguments:
- fitted_tensor: bfloat16 [4, 8192, 8192], P('grp', 'aux', 'orb'), may hold values from -0.23925781 to 0.23925781
- block_mask: int32 [2, 64, 64], P('grp'), may hold values 0 or 1
- orbitals: bfloat16 [8192, 256], P('aux'), may hold values from -0.0625 to 0.0625
- nuclear: float32 [8192], replicated, may hold values from 0.5 to 1.5
- centres: float32 [3, 8192], replicated, may hold values from 0 to 8
- mm_positions: float32 [3, 32768], P(None, ('grp', 'aux', 'orb')), may hold values from 0 to 8
- mm_charges: float32 [32768], P(('grp', 'aux', 'orb')), may hold values from -0.12 to 0.12
- neighbours: int32 [32, 2], P(('grp', 'aux', 'orb')), may hold values from 0 to 63, all different within a row
Outputs:
- fock: float32 [8192, 8192], P(('aux', 'orb'))
- mm_potential: float32 [32768], P(('grp', 'aux', 'orb'))
Inputs may be any that keep to these rules, and one draw needn't show every extreme that they name: `neighbours`: each row names 2 different blocks; every block is named by some row.
All inputs are finite; a program needn't handle non-finite values. No bound on the sum of `block_mask` on one device may be relied on, other than what follows from the above.
Results may differ from a plain program's by a relative error of at most 0.01.
Values may be sent and summed in bfloat16 or wider, within the bound.
A program may use at most 128 MiB of HBM per device.

v0:
```python
import jax
import jax.numpy as jnp
from jax import lax
from jax.sharding import PartitionSpec as P

BLK = 128
softening = 1.0


def near_kernel(picker, centre_blocks, charge_blocks, atom_xyz):
    near_xyz = jnp.einsum("kb,cbj->ckj", picker, centre_blocks, precision=lax.Precision.HIGHEST)
    near_xyz = near_xyz.reshape(3, picker.shape[0] * centre_blocks.shape[2])
    near_q = jnp.dot(picker, charge_blocks, precision=lax.Precision.HIGHEST).reshape(-1)
    offsets = near_xyz[:, :, None] - atom_xyz[:, None, :]
    kernel = lax.rsqrt(jnp.sum(offsets * offsets, axis=0) + softening)
    return (kernel, near_q)


def add_diagonal(fock_rows, first_row, field_vec):
    row_count = fock_rows.shape[0]
    values = lax.dynamic_slice_in_dim(field_vec, first_row, row_count, 0)
    row_ids = jnp.arange(row_count, dtype=jnp.int32)[:, None]
    col_ids = jnp.arange(fock_rows.shape[1], dtype=jnp.int32)[None, :]
    on_diagonal = col_ids == first_row + row_ids
    return fock_rows + jnp.where(on_diagonal, values[:, None], jnp.float32(0.0))


def block_picker(first, count, block_total):
    positions = (first + jnp.arange(count, dtype=jnp.int32)) // BLK
    block_ids = jnp.arange(block_total, dtype=jnp.int32)
    return (positions[:, None] == block_ids[None, :]).astype(jnp.float32)


def per_device(
    fitted_tensor, block_mask, orbitals, nuclear, centres, mm_positions, mm_charges, neighbours
):
    row_span = fitted_tensor.shape[1]
    col_span = fitted_tensor.shape[2]
    orb_count = lax.axis_size("orb")
    aux_id = lax.axis_index("aux")
    orb_id = lax.axis_index("orb")
    own_span = row_span // orb_count
    block_total = block_mask.shape[1]
    whole_c = lax.all_gather(orbitals, "aux", axis=0, tiled=True)
    row_start = aux_id * row_span
    col_start = orb_id * col_span
    window_c = lax.dynamic_slice_in_dim(whole_c, col_start, col_span, 0)
    row_pick = block_picker(row_start, row_span, block_total)
    col_pick = block_picker(col_start, col_span, block_total)
    row_bits = jnp.dot(row_pick, block_mask[0].astype(jnp.float32), precision=lax.Precision.HIGHEST)
    mask_wide = jnp.dot(row_bits, col_pick.T, precision=lax.Precision.HIGHEST).astype(jnp.bfloat16)
    masked = fitted_tensor * mask_wide[None]
    x_partial = jnp.einsum("pmn,ni->pmi", masked, window_c, preferred_element_type=jnp.float32)
    x_rows = lax.psum(x_partial, "orb")
    own_rows = lax.dynamic_slice_in_dim(x_rows, orb_id * own_span, own_span, 1)
    x_own = own_rows.astype(jnp.bfloat16)
    own_c = lax.dynamic_slice_in_dim(orbitals, orb_id * own_span, own_span, 0)
    dens_part = 2.0 * jnp.einsum("pmi,mi->p", x_own, own_c, preferred_element_type=jnp.float32)
    densities = lax.psum(dens_part, ("aux", "orb")).astype(jnp.bfloat16)
    coulomb_block = jnp.einsum("pmn,p->mn", masked, densities, preferred_element_type=jnp.float32)
    coulomb = lax.all_to_all(coulomb_block, "orb", split_axis=0, concat_axis=1, tiled=True)
    c_float = whole_c.astype(jnp.float32)
    population = 2.0 * jnp.sum(c_float * c_float, axis=1)
    qm_charge = nuclear - population
    centre_blocks = centres.reshape(3, block_total, BLK)
    charge_blocks = qm_charge.reshape(block_total, BLK)
    picker = (neighbours[0][:, None] == jnp.arange(block_total, dtype=jnp.int32)[None, :]).astype(
        jnp.float32
    )
    kernel, near_q = near_kernel(picker, centre_blocks, charge_blocks, mm_positions)
    mm_potential = jnp.dot(near_q, kernel, precision=lax.Precision.HIGHEST)
    contrib = jnp.dot(kernel, mm_charges, precision=lax.Precision.HIGHEST).reshape(
        picker.shape[0], BLK
    )
    field_part = jnp.dot(picker.T, contrib, precision=lax.Precision.HIGHEST)
    field_sum = lax.psum(field_part, ("grp", "aux", "orb"))
    field_vec = field_sum.reshape(-1)
    own_first = row_start + orb_id * own_span
    exchange_part = jnp.einsum(
        "pmi,pni->mn",
        x_own,
        lax.all_gather(x_own, ("aux", "orb"), axis=1, tiled=True),
        preferred_element_type=jnp.float32,
    )
    fock_part = coulomb - 0.5 * exchange_part
    fock_sum = lax.psum(fock_part, "grp")
    fock = add_diagonal(fock_sum, own_first, field_vec)
    return (fock, mm_potential)


def solution(mesh):
    in_specs = (
        P("grp", "aux", "orb"),
        P("grp", None, None),
        P("aux", None),
        P(),
        P(),
        P(None, ("grp", "aux", "orb")),
        P(("grp", "aux", "orb")),
        P(("grp", "aux", "orb"), None),
    )
    out_specs = (P(("aux", "orb"), None), P(("grp", "aux", "orb")))
    return jax.shard_map(
        per_device, mesh=mesh, in_specs=in_specs, out_specs=out_specs, check_vma=False
    )
```

profile of v0, /device:TPU:0, one launch (start us, length us, event | category | flops | bytes accessed | tf_op | source)
XLA Modules:
  0.0 848.3 jit_solution(9946186388667584154)
XLA Ops:
  7.2 0.0 copy-start
  7.2 0.0 all-gather.3.cloned.1.call-start
  7.2 0.7 all-gather.3.cloned.1.call-update
  8.0 1.0 bitcast_convert_fusion
  9.0 1.7 fusion.6
  10.6 7.5 convolution_convert_fusion
  18.1 14.8 %broadcast_multiply_fusion = bf16[2,2048,2048]{2,1,0:T(8,128)(2,1)} fusion(bf16[2,2048,2048]{2,1,0:T(8,128)(2,1)} %param.8, bf16[2048,2048]{1,0:T(8,128)(2,1)S(1)} %convolution_convert_fusion), kind=kLoop, calls=%fused_computation.7 | loop fusion | flops 8388608 | bytes 41943040 | tf_op jit(solution)/shard_map/mul | solution.py:52
  32.9 32.4 %all-gather.3.cloned.1.call-done = bf16[8192,256]{1,0:T(8,128)(2,1)} async-done(((bf16[2048,256]{1,0:T(8,128)(2,1)}), bf16[8192,256]{1,0:T(8,128)(2,1)}) %all-gather.3.cloned.1.call-update) | async-done | bytes 4194320 | tf_op jit(solution)/shard_map/all_gather | solution.py:44
  65.3 12.5 %fusion.3 = f32[2,2048,256]{2,1,0:T(8,128)} fusion(bf16[2,2048,2048]{2,1,0:T(8,128)(2,1)} %broadcast_multiply_fusion, bf16[8192,256]{1,0:T(8,128)(2,1)} %all-gather.3.cloned.1.call-done, s32[]{:T(128)S(6)} %select_n.32), kind=kOutput, calls=%fused_computation.12 | convolution fusion | flops 4294967296 | bytes 22020100 | tf_op jit(solution)/shard_map/pmn,ni->pmi/dot_general | solution.py:53
  77.8 147.1 %all-reduce.4 = bf16[2,2048,256]{2,1,0:T(8,128)(2,1)S(1)} all-reduce(f32[2,2048,256]{2,1,0:T(8,128)} %fusion.3), channel_id=1, replica_groups=mesh['grp'=2,'aux'=4,'orb'=4] {'orb'}, use_global_device_ids=true, to_apply=%region_0.1 | all-reduce | flops 1048576 | bytes 6291456 | tf_op jit(solution)/shard_map/psum | solution.py:54
  224.9 1.0 multiply_reduce_fusion.2
  225.9 38.2 %psum.29 = bf16[2]{0:T(256)(128)(2,1)S(1)} all-reduce(f32[2]{0:T(128)S(1)} %broadcast_multiply_fusion.1), channel_id=1, replica_groups=mesh['grp'=2,'aux'=4,'orb'=4] {'aux','orb'}, use_global_device_ids=true, to_apply=%region_1.2 | all-reduce | flops 2 | bytes 12 | tf_op jit(solution)/shard_map/psum | solution.py:59
  264.2 28.8 %fusion.1 = f32[1,2048,2048]{2,0,1:T(1,128)S(1)} fusion(bf16[2,2048,2048]{2,1,0:T(8,128)(2,1)} %broadcast_multiply_fusion, bf16[2]{0:T(256)(128)(2,1)S(1)} %psum.29), kind=kOutput, calls=%fused_computation.4 | convolution fusion | flops 16777216 | bytes 33554436 | tf_op jit(solution)/shard_map/pmn,p->mn/dot_general | solution.py:60
  292.9 11.3 %copy.18 = f32[1,2048,2048]{2,1,0:T(8,128)} copy(f32[1,2048,2048]{2,0,1:T(1,128)S(1)} %fusion.1) | data formatting | bytes 33554432 | tf_op jit(solution)/shard_map/pmn,p->mn/dot_general | solution.py:60
  304.2 7.0 all-to-all-start
  311.2 0.0 all-gather.5.cloned.1.call-start
  311.2 0.7 all-gather.5.cloned.1.call-update
  312.0 0.0 all-reduce.3.cloned.1.call-start
  312.0 433.2 %all-to-all-done = f32[4,512,2048]{2,1,0:T(8,128)} async-done(((f32[4,512,2048]{2,1,0:T(8,128)}), f32[4,512,2048]{2,1,0:T(8,128)}, u32[]{:S(2)}, u32[]{:S(2)}) %all-to-all-start) | async-done | bytes 16777248 | tf_op jit(solution)/shard_map/all_to_all | solution.py:61
  745.2 0.0 copy-start.1
  745.2 11.9 %copy.21 = f32[4,64,8,2048]{3,2,0,1:T(8,128)} copy(f32[4,64,8,2048]{3,2,1,0:T(8,128)} %bitcast.23) | data formatting | bytes 33554432 | tf_op jit(solution)/shard_map/all_to_all | solution.py:61
  757.0 0.0 all-gather.5.cloned.1.call-done
  757.0 0.0 copy-done.1
  757.0 14.4 %fusion = f32[512,8192]{1,0:T(8,128)} fusion(f32[512,8192]{1,0:T(8,128)} %bitcast.59, bf16[2,512,256]{2,1,0:T(8,128)(2,1)S(1)} %copy-done.1, bf16[2,8192,256]{2,1,0:T(8,128)(2,1)} %all-gather.5.cloned.1.call-done), kind=kOutput, calls=%fused_computation.1 | convolution fusion | flops 4303355904 | bytes 42467328 | tf_op jit(solution)/shard_map/pmi,pni->mn/dot_general | solution.py:79
  771.4 0.0 copy-start.2
  771.4 0.0 copy-start.5
  771.4 0.0 copy-start.4
  771.4 0.0 copy-start.3
  771.5 0.0 all-reduce.3.cloned.1.call-update
  771.5 0.9 copy-done.2
  772.3 0.0 copy-done.5
  772.3 0.2 convolution_bitcast_fusion.1
  772.5 0.0 copy-done.4
  772.5 0.4 multiply_reduce_fusion.1
  772.9 0.0 copy-done
  772.9 1.0 fusion.8
  773.9 0.3 convolution_bitcast_fusion
  774.2 37.3 %psum.31 = f32[8192]{0:T(1024)S(1)} all-reduce(f32[8192]{0:T(1024)S(1)} %convolution_bitcast_fusion), channel_id=1, replica_groups=mesh['grp'=2,'aux'=4,'orb'=4] {'grp','aux','orb'}, use_global_device_ids=true, to_apply=%region_4.5 | all-reduce | flops 8192 | bytes 65536 | tf_op jit(solution)/shard_map/psum | solution.py:76
  811.5 0.1 dynamic_slice.15
  811.6 3.8 multiply_reduce_fusion
  815.3 0.0 copy-done.3
  815.3 0.2 fusion.15
  815.5 1.3 fusion.7
  816.8 12.9 %all-reduce.3.cloned.1.call-done = f32[512,8192]{1,0:T(8,128)} async-done(((f32[512,8192]{1,0:T(8,128)}), f32[512,8192]{1,0:T(8,128)}) %all-reduce.3.cloned.1.call-update) | async-done | bytes 16777232 | tf_op jit(solution)/shard_map/psum | solution.py:86
  829.7 12.1 %select_add_fusion = f32[512,8192]{1,0:T(8,128)} fusion(f32[512,8192]{1,0:T(8,128)} %all-reduce.3.cloned.1.call-done, f32[512]{0:T(512)S(1)} %dynamic_slice.15, s32[512]{0:T(512)S(1)} %iota_add_fusion.2), kind=kLoop, calls=%fused_computation.2 | loop fusion | flops 12582912 | bytes 33558528 | tf_op jit(solution)/shard_map/add | solution.py:25
  (5 shorter events, 0.0 us)
Async XLA Ops:
  7.2 765.8 %copy-start = (f32[1024]{0:T(1024)S(1)}, f32[1024]{0:T(1024)}, u32[]{:S(2)}) copy-start(f32[1024]{0:T(1024)} %param.14) | copy-start | bytes 12292
  7.2 58.1 %all-gather.3.cloned.1.call-start = ((), (), s32[]{:S(2)}) async-start(), calls=%async_computation.1 | async-start | bytes 5242880 | tf_op jit(solution)/shard_map/all_gather | solution.py:44
  304.2 440.9 %all-to-all-start = ((f32[4,512,2048]{2,1,0:T(8,128)}), f32[4,512,2048]{2,1,0:T(8,128)}, u32[]{:S(2)}, u32[]{:S(2)}) async-start(f32[4,512,2048]{2,1,0:T(8,128)} %bitcast.58), calls=%async_computation | async-start | bytes 33554432 | tf_op jit(solution)/shard_map/all_to_all | solution.py:61
  311.2 445.8 %all-gather.5.cloned.1.call-start = ((), (), s32[]{:S(2)}) async-start(), calls=%async_computation.2 | async-start | bytes 8912896 | tf_op jit(solution)/shard_map/all_gather | solution.py:82
  312.0 517.8 %all-reduce.3.cloned.1.call-start = ((), (), s32[]{:S(2)}) async-start(), calls=%async_computation.3 | async-start | bytes 33554432 | tf_op jit(solution)/shard_map/psum | solution.py:86
  745.2 11.9 %copy-start.1 = (bf16[2,512,256]{2,1,0:T(8,128)(2,1)S(1)}, bf16[2,512,256]{2,1,0:T(8,128)(2,1)}, u32[]{:S(2)}) copy-start(bf16[2,512,256]{2,1,0:T(8,128)(2,1)} %get-tuple-element.3) | copy-start | bytes 1572868
  771.4 0.9 copy-start.2
  771.4 0.9 copy-start.5
  771.4 1.1 copy-start.4
  771.4 43.9 %copy-start.3 = (f32[8192]{0:T(1024)S(1)}, f32[8192]{0:T(1024)}, u32[]{:S(2)}) copy-start(f32[8192]{0:T(1024)} %param.11) | copy-start | bytes 98308
Sparse Core Ops, SparseCore 0:
  9.9 55.3 all-gather.2
  314.8 381.6 all-gather.4
  771.6 58.0 all-reduce.2
where the time goes:
time: 849 us; the launch traced here: 848 us
  waiting for transfers between devices  480 us (57%)
  blocking collectives  223 us (26%)
  matrix products  67.7 us (8%)
  other arithmetic  33.1 us (4%)
  local copies, waits for them, and re-layouts  24.2 us (3%)
  between operations  13.9 us (2%)
    all_to_all x1, waiting for transfers between devices, per_device(): lax.all_to_all(coulomb_block, 'orb', split_axis=0, concat_axis=1, tiled=T...  433 us
    psum x1, blocking collectives, per_device(): x_rows = lax.psum(x_partial, 'orb')  147 us
    psum x1, blocking collectives, per_device(): densities = lax.psum(dens_part, ('aux', 'orb')).astype(jnp.bfloat16)  38.2 us
    psum x1, blocking collectives, per_device(): field_sum = lax.psum(field_part, ('grp', 'aux', 'orb'))  37.3 us
    all_gather x1, waiting for transfers between devices, per_device(): whole_c = lax.all_gather(orbitals, 'aux', axis=0, tiled=True)  32.4 us
    dot_general x1, matrix products, per_device(): jnp.einsum('pmn,p->mn', masked, densities, preferred_element_type=jnp.flo...  28.8 us
  transfers between devices with their start and end apart: 4, of which 3 were waited for; matrix products, arithmetic and copies ran while one was open for 5% of the time, Pallas kernels for 0%

commit v1 on v0

--- a/solution.py
+++ b/solution.py
@@ -58,7 +58,10 @@
     dens_part = 2.0 * jnp.einsum("pmi,mi->p", x_own, own_c, preferred_element_type=jnp.float32)
     densities = lax.psum(dens_part, ("aux", "orb")).astype(jnp.bfloat16)
     coulomb_block = jnp.einsum("pmn,p->mn", masked, densities, preferred_element_type=jnp.float32)
-    coulomb = lax.all_to_all(coulomb_block, "orb", split_axis=0, concat_axis=1, tiled=True)
+    r_now = jnp.split(coulomb_block, jax.lax.axis_size("orb"), 0)
+    coulomb = jnp.concatenate(
+        jax.lax.all_to_all(jnp.stack(r_now, 0), split_axis=0, axis_name="orb", concat_axis=0), 1
+    )
     c_float = whole_c.astype(jnp.float32)
     population = 2.0 * jnp.sum(c_float * c_float, axis=1)
     qm_charge = nuclear - population

time: 849 us -> 917 us (1.080)
  matrix products: 67.7 us -> 121 us
  other arithmetic: 33.1 us -> 43.9 us
    dot_general x1, matrix products: 28.8 us -> 81.8 us  [per_device(): jnp.einsum('pmn,p->mn', masked, densities, preferred_element_type=jnp.flo...]
    all_to_all x1 -> x0, local copies, waits for them, and re-layouts: 11.9 us -> none  [per_device(): lax.all_to_all(coulomb_block, 'orb', split_axis=0, concat_axis=1, tiled=T...]
    reshape x0 -> x1, local copies, waits for them, and re-layouts: none -> 11.9 us  [per_device(): jnp.concatenate(jax.lax.all_to_all(jnp.stack(r_now, 0), split_axis=0, axi...]
    another operation x0 -> x1, other arithmetic: none -> 10.9 us  [per_device(): jnp.stack(r_now, 0)]
where the time goes in v1:
time: 917 us
  waiting for transfers between devices  480 us (52%)
  blocking collectives  222 us (24%)
  matrix products  121 us (13%)
  other arithmetic  43.9 us (5%)
  local copies, waits for them, and re-layouts  28.5 us (3%)
  between operations  13.9 us (2%)
    all_to_all x1, waiting for transfers between devices, per_device(): jax.lax.all_to_all(jnp.stack(r_now, 0), split_axis=0, axis_name='orb', co...  433 us
    psum x1, blocking collectives, per_device(): x_rows = lax.psum(x_partial, 'orb')  147 us
    dot_general x1, matrix products, per_device(): jnp.einsum('pmn,p->mn', masked, densities, preferred_element_type=jnp.flo...  81.8 us
    psum x1, blocking collectives, per_device(): densities = lax.psum(dens_part, ('aux', 'orb')).astype(jnp.bfloat16)  38.2 us
    psum x1, blocking collectives, per_device(): field_sum = lax.psum(field_part, ('grp', 'aux', 'orb'))  37.1 us
    all_gather x1, waiting for transfers between devices, per_device(): whole_c = lax.all_gather(orbitals, 'aux', axis=0, tiled=True)  32.4 us
  transfers between devices with their start and end apart: 4, of which 3 were waited for; matrix products, arithmetic and copies ran while one was open for 5% of the time, Pallas kernels for 0%

profile of v1, /device:TPU:0, one launch (start us, length us, event | category | flops | bytes accessed | tf_op | source)
XLA Modules:
  0.0 916.6 jit_solution(322418526010316319)
XLA Ops:
  7.2 0.0 copy-start
  7.2 0.0 all-gather.3.cloned.1.call-start
  7.2 0.7 all-gather.3.cloned.1.call-update
  8.0 1.0 bitcast_convert_fusion
  9.0 1.7 fusion.6
  10.6 7.5 convolution_convert_fusion
  18.1 14.8 %broadcast_multiply_fusion = bf16[2,2048,2048]{2,1,0:T(8,128)(2,1)} fusion(bf16[2,2048,2048]{2,1,0:T(8,128)(2,1)} %param.8, bf16[2048,2048]{1,0:T(8,128)(2,1)S(1)} %convolution_convert_fusion), kind=kLoop, calls=%fused_computation.9 | loop fusion | flops 8388608 | bytes 41943040 | tf_op jit(solution)/shard_map/mul | solution.py:52
  32.9 32.4 %all-gather.3.cloned.1.call-done = bf16[8192,256]{1,0:T(8,128)(2,1)} async-done(((bf16[2048,256]{1,0:T(8,128)(2,1)}), bf16[8192,256]{1,0:T(8,128)(2,1)}) %all-gather.3.cloned.1.call-update) | async-done | bytes 4194320 | tf_op jit(solution)/shard_map/all_gather | solution.py:44
  65.3 12.5 %fusion.3 = f32[2,2048,256]{2,1,0:T(8,128)} fusion(bf16[2,2048,2048]{2,1,0:T(8,128)(2,1)} %broadcast_multiply_fusion, bf16[8192,256]{1,0:T(8,128)(2,1)} %all-gather.3.cloned.1.call-done, s32[]{:T(128)S(6)} %select_n.32), kind=kOutput, calls=%fused_computation.18 | convolution fusion | flops 4294967296 | bytes 22020100 | tf_op jit(solution)/shard_map/pmn,ni->pmi/dot_general | solution.py:53
  77.8 147.1 %all-reduce.4 = bf16[2,2048,256]{2,1,0:T(8,128)(2,1)S(1)} all-reduce(f32[2,2048,256]{2,1,0:T(8,128)} %fusion.3), channel_id=1, replica_groups=mesh['grp'=2,'aux'=4,'orb'=4] {'orb'}, use_global_device_ids=true, to_apply=%region_0.1 | all-reduce | flops 1048576 | bytes 6291456 | tf_op jit(solution)/shard_map/psum | solution.py:54
  224.9 1.0 multiply_reduce_fusion.2
  225.9 38.2 %psum.29 = bf16[2]{0:T(256)(128)(2,1)S(1)} all-reduce(f32[2]{0:T(128)S(1)} %broadcast_multiply_fusion.1), channel_id=1, replica_groups=mesh['grp'=2,'aux'=4,'orb'=4] {'aux','orb'}, use_global_device_ids=true, to_apply=%region_1.2 | all-reduce | flops 2 | bytes 12 | tf_op jit(solution)/shard_map/psum | solution.py:59
  264.2 81.8 %fusion.1 = f32[1,2048,2048]{2,0,1:T(1,128)} fusion(bf16[2,2048,2048]{2,1,0:T(8,128)(2,1)} %broadcast_multiply_fusion, bf16[2]{0:T(256)(128)(2,1)S(1)} %psum.29), kind=kOutput, calls=%fused_computation.6 | convolution fusion | flops 16777216 | bytes 33554436 | tf_op jit(solution)/shard_map/pmn,p->mn/dot_general | solution.py:60
  346.0 11.0 %copy.35 = f32[1,2048,2048]{2,1,0:T(8,128)S(1)} copy(f32[1,2048,2048]{2,0,1:T(1,128)} %fusion.1) | data formatting | bytes 33554432 | tf_op jit(solution)/shard_map/pmn,p->mn/dot_general | solution.py:60
  357.0 4.6 slice_bitcast_fusion.3
  361.6 10.9 %pad_maximum_fusion = f32[4,512,2048]{2,1,0:T(8,128)} fusion(f32[1,512,2048]{2,1,0:T(8,128)} %get-tuple-element.5, f32[1,512,2048]{2,1,0:T(8,128)} %get-tuple-element.6, f32[1,512,2048]{2,1,0:T(8,128)} %get-tuple-element.7, f32[1,512,2048]{2,1,0:T(8,128)S(1)} %get-tuple-element.4), kind=kLoop, calls=%fused_computation | loop fusion | flops 12582912 | bytes 33554432 | tf_op jit(solution)/shard_map/stack | solution.py:63
  372.4 7.0 all-to-all-start
  379.4 0.0 all-gather.5.cloned.1.call-start
  379.5 0.7 all-gather.5.cloned.1.call-update
  380.2 0.3 all-reduce.3.cloned.1.call-start
  380.4 432.9 %all-to-all-done = f32[4,512,2048]{2,1,0:T(8,128)} async-done(((f32[4,512,2048]{2,1,0:T(8,128)}), f32[4,512,2048]{2,1,0:T(8,128)}, u32[]{:S(2)}, u32[]{:S(2)}) %all-to-all-start) | async-done | bytes 16777248 | tf_op jit(solution)/shard_map/all_to_all | solution.py:63
  813.4 0.0 copy-start.1
  813.4 11.9 %copy.24 = f32[4,64,8,2048]{3,2,0,1:T(8,128)} copy(f32[4,64,8,2048]{3,2,1,0:T(8,128)} %bitcast.25) | data formatting | bytes 33554432 | tf_op jit(solution)/shard_map/reshape | solution.py:62
  825.2 0.0 all-gather.5.cloned.1.call-done
  825.3 0.0 copy-done.1
  825.3 14.4 %fusion = f32[512,8192]{1,0:T(8,128)} fusion(f32[512,8192]{1,0:T(8,128)} %bitcast.67, bf16[2,512,256]{2,1,0:T(8,128)(2,1)S(1)} %copy-done.1, bf16[2,8192,256]{2,1,0:T(8,128)(2,1)} %all-gather.5.cloned.1.call-done), kind=kOutput, calls=%fused_computation.2 | convolution fusion | flops 4303355904 | bytes 42467328 | tf_op jit(solution)/shard_map/pmi,pni->mn/dot_general | solution.py:82
  839.6 0.0 copy-start.2
  839.6 0.0 copy-start.5
  839.6 0.0 copy-start.4
  839.6 0.0 copy-start.3
  839.7 0.0 all-reduce.3.cloned.1.call-update
  839.7 0.9 copy-done.2
  840.5 0.0 copy-done.5
  840.5 0.2 convolution_bitcast_fusion.1
  840.7 0.0 copy-done.4
  840.8 0.4 multiply_reduce_fusion.1
  841.1 0.0 copy-done
  841.1 1.0 fusion.8
  842.1 0.3 convolution_bitcast_fusion
  842.4 37.1 %psum.31 = f32[8192]{0:T(1024)S(1)} all-reduce(f32[8192]{0:T(1024)S(1)} %convolution_bitcast_fusion), channel_id=1, replica_groups=mesh['grp'=2,'aux'=4,'orb'=4] {'grp','aux','orb'}, use_global_device_ids=true, to_apply=%region_4.5 | all-reduce | flops 8192 | bytes 65536 | tf_op jit(solution)/shard_map/psum | solution.py:79
  879.5 0.1 dynamic_slice.15
  879.6 3.7 multiply_reduce_fusion
  883.3 0.0 copy-done.3
  883.3 0.2 fusion.15
  883.5 1.3 fusion.7
  884.7 13.2 %all-reduce.3.cloned.1.call-done = f32[512,8192]{1,0:T(8,128)} async-done(((f32[512,8192]{1,0:T(8,128)}), f32[512,8192]{1,0:T(8,128)}) %all-reduce.3.cloned.1.call-update) | async-done | bytes 16777232 | tf_op jit(solution)/shard_map/psum | solution.py:89
  898.0 12.1 %select_add_fusion = f32[512,8192]{1,0:T(8,128)} fusion(f32[512,8192]{1,0:T(8,128)} %all-reduce.3.cloned.1.call-done, f32[512]{0:T(512)S(1)} %dynamic_slice.15, s32[512]{0:T(512)S(1)} %iota_add_fusion.2), kind=kLoop, calls=%fused_computation.4 | loop fusion | flops 12582912 | bytes 33558528 | tf_op jit(solution)/shard_map/add | solution.py:25
  (5 shorter events, 0.0 us)
Async XLA Ops:
  7.2 834.0 %copy-start = (f32[1024]{0:T(1024)S(1)}, f32[1024]{0:T(1024)}, u32[]{:S(2)}) copy-start(f32[1024]{0:T(1024)} %param.14) | copy-start | bytes 12292
  7.2 58.1 %all-gather.3.cloned.1.call-start = ((), (), s32[]{:S(2)}) async-start(), calls=%async_computation.1 | async-start | bytes 5242880 | tf_op jit(solution)/shard_map/all_gather | solution.py:44
  372.4 440.9 %all-to-all-start = ((f32[4,512,2048]{2,1,0:T(8,128)}), f32[4,512,2048]{2,1,0:T(8,128)}, u32[]{:S(2)}, u32[]{:S(2)}) async-start(f32[4,512,2048]{2,1,0:T(8,128)} %pad_maximum_fusion), calls=%async_computation | async-start | bytes 33554432 | tf_op jit(solution)/shard_map/all_to_all | solution.py:63
  379.4 445.8 %all-gather.5.cloned.1.call-start = ((), (), s32[]{:S(2)}) async-start(), calls=%async_computation.2 | async-start | bytes 8912896 | tf_op jit(solution)/shard_map/all_gather | solution.py:85
  380.2 517.8 %all-reduce.3.cloned.1.call-start = ((), (), s32[]{:S(2)}) async-start(), calls=%async_computation.3 | async-start | bytes 33554432 | tf_op jit(solution)/shard_map/psum | solution.py:89
  813.4 11.9 %copy-start.1 = (bf16[2,512,256]{2,1,0:T(8,128)(2,1)S(1)}, bf16[2,512,256]{2,1,0:T(8,128)(2,1)}, u32[]{:S(2)}) copy-start(bf16[2,512,256]{2,1,0:T(8,128)(2,1)} %get-tuple-element.3) | copy-start | bytes 1572868
  839.6 0.9 copy-start.2
  839.6 0.9 copy-start.5
  839.6 1.1 copy-start.4
  839.6 43.6 %copy-start.3 = (f32[8192]{0:T(1024)S(1)}, f32[8192]{0:T(1024)}, u32[]{:S(2)}) copy-start(f32[8192]{0:T(1024)} %param.11) | copy-start | bytes 98308
Sparse Core Ops, SparseCore 0:
  9.9 55.3 all-gather.2
  383.0 381.6 all-gather.4
  839.8 58.1 all-reduce.2
